TPU v7x, 32 devices: a whole 2x2x4 slice. The times are simulated.
32 devices in a mesh: row: 8 (over z, x), col: 4 (over y, core).
Axes of the slice: x: 2, y: 2, z: 4, core: 2. Of those that a mesh axis runs over, the one named last changes fastest.
Arguments:
- records: bfloat16 [128, 8, 1500], P('row', 'col'), may hold values from -6 to 6
- channel_live: int32 [128], replicated, may hold values 0 or 1
- minute_valid: int32 [8], replicated, may hold values 0 or 1
Outputs:
- correlations: bfloat16 [128, 128, 801], P('row', 'col')
All inputs are finite; a program needn't handle non-finite values.
Results may differ from a plain program's by a relative error of at most 0.0075.
Values may be sent and summed in bfloat16 or wider, within the bound.
A program may use at most 64 MiB of HBM per device.

v0:
```python
import math

import jax
import jax.numpy as jnp
from jax import lax
from jax.sharding import PartitionSpec as P

F = 640
BAND = 32
MAXLAG = 400


def forward_table(length, nfreq):
    times = jnp.arange(length, dtype=jnp.int32)[:, None]
    freqs = jnp.arange(1, nfreq + 1, dtype=jnp.int32)[None, :]
    phase = (times * freqs % length).astype(jnp.float32) * jnp.float32(2.0 * math.pi / length)
    return jnp.concatenate([jnp.cos(phase), -jnp.sin(phase)], axis=1).astype(jnp.bfloat16)


def inverse_table(length, nfreq, maxlag):
    freqs = jnp.arange(1, nfreq + 1, dtype=jnp.int32)[:, None]
    shifts = jnp.arange(-maxlag, maxlag + 1, dtype=jnp.int32)[None, :]
    phase = jnp.mod(freqs * shifts, length).astype(jnp.float32) * jnp.float32(
        2.0 * math.pi / length
    )
    return jnp.concatenate([jnp.cos(phase), -jnp.sin(phase)], axis=0).astype(jnp.bfloat16)


def whiten(signal, live, valid, table, band):
    chans, mins, length = signal.shape
    nfreq = table.shape[1] // 2
    spectrum = jnp.dot(
        signal.reshape(chans * mins, length), table, preferred_element_type=jnp.float32
    )
    grouped = spectrum.reshape(chans, mins, 2, nfreq // band, band)
    power = jnp.mean(grouped * grouped, axis=(2, 4))
    weight = (
        lax.rsqrt(power + 1e-06)
        * live.astype(jnp.float32)[:, None, None]
        * valid.astype(jnp.float32)[None, :, None]
    )
    return (
        (grouped * weight[:, :, None, :, None]).reshape(chans, mins, 2 * nfreq).astype(jnp.bfloat16)
    )


def correlate(rows, cols, itab, count):
    nfreq = rows.shape[2] // 2
    row_real = rows[:, :, :nfreq]
    row_imag = rows[:, :, nfreq:]
    col_real = cols[:, :, :nfreq]
    col_imag = cols[:, :, nfreq:]
    real_sum = jnp.einsum(
        "imf,jmf->ijf", row_real, col_real, preferred_element_type=jnp.float32
    ) + jnp.einsum("imf,jmf->ijf", row_imag, col_imag, preferred_element_type=jnp.float32)
    imag_sum = jnp.einsum(
        "imf,jmf->ijf", row_imag, col_real, preferred_element_type=jnp.float32
    ) - jnp.einsum("imf,jmf->ijf", row_real, col_imag, preferred_element_type=jnp.float32)
    stacked = (jnp.concatenate([real_sum, imag_sum], axis=-1) / jnp.float32(count)).astype(
        jnp.bfloat16
    )
    lagged = jnp.dot(stacked.reshape(-1, 2 * nfreq), itab, preferred_element_type=jnp.float32)
    lagged = lagged * jnp.float32(1.0 / math.sqrt(nfreq))
    return lagged.astype(jnp.bfloat16).reshape(rows.shape[0], cols.shape[0], itab.shape[1])


def body(records, channel_live, minute_valid):
    row_total = lax.axis_size("row")
    col_total = lax.axis_size("col")
    row_count = records.shape[0]
    per_device = records.shape[1]
    length = records.shape[2]
    channels = row_count * row_total
    col_count = channels // col_total
    minutes = per_device * col_total
    col_index = lax.axis_index("col")
    row_start = lax.axis_index("row") * row_count
    row_live = lax.dynamic_slice_in_dim(channel_live, row_start, row_count)
    table = forward_table(length, F)
    own_valid = lax.dynamic_slice_in_dim(minute_valid, col_index * per_device, per_device)
    local = whiten(records, row_live, own_valid, table, BAND)
    row_spectra = lax.all_gather(local, "col", axis=1, tiled=True)
    every_channel = lax.all_gather(local, "row", axis=0, tiled=True)
    col_spectra = lax.all_to_all(every_channel, "col", split_axis=0, concat_axis=1, tiled=True)
    itab = inverse_table(length, F, MAXLAG)
    block = math.gcd(row_count, 8)
    grouped = row_spectra.reshape(row_count // block, block, minutes, 2 * F)

    def one_block(rows):
        return correlate(rows, col_spectra, itab, minutes)

    result = lax.map(one_block, grouped)
    return result.reshape(row_count, col_count, 2 * MAXLAG + 1)


def solution(mesh):
    in_specs = (P("row", "col", None), P(), P())
    out_specs = P("row", "col", None)
    return jax.shard_map(body, mesh=mesh, in_specs=in_specs, out_specs=out_specs, check_vma=False)
```

profile of v0, /device:TPU:0, one launch (start us, length us, event | category | flops | bytes accessed | tf_op | source)
XLA Modules:
  0.0 129.4 jit_solution(9751996412103795063)
XLA Ops:
  0.0 17.2 %cosine_convert_fusion = (bf16[1500,640]{1,0:T(8,128)(2,1)S(1)}, bf16[1500,640]{1,0:T(8,128)(2,1)}) fusion(s32[640]{0:T(1024)S(1)} %iota_add_fusion.1), kind=kLoop, calls=%fused_computation.31 | loop fusion | flops 11520000 | bytes 3842560 | tf_op jit(solution)/shard_map/convert.2
  17.3 2.3 %fusion.45 = (f32[32,1280]{1,0:T(8,128)S(1)}, f32[32,1280]{1,0:T(8,128)S(1)}) fusion(bf16[32,1500]{1,0:T(8,128)(2,1)S(1)} %reshape.42, bf16[1500,640]{1,0:T(8,128)(2,1)} %get-tuple-element.61, bf16[1500,640]{1,0:T(8,128)(2,1)S(1)} %get-tuple-element.60), kind=kOutput, calls=%fused_computation.59 | convolution fusion | flops 130600960 | bytes 4263680 | tf_op jit(solution)/shard_map/dot_general | solution.py:32
  19.6 0.3 mul.110
  20.0 0.2 reduce_sum.9
  20.3 0.2 mul.117
  20.5 0.3 mul.118
  20.8 0.1 reshape.43
  20.9 33.5 %all_gather.7 = bf16[128,2,1280]{2,0,1:T(8,128)(2,1)S(1)} all-gather(bf16[16,2,1280]{2,0,1:T(8,128)(2,1)S(1)} %fusion.39), channel_id=1, replica_groups=mesh['row'=8,'col'=4] {'row'}, dimensions={0}, use_global_device_ids=true | all-gather | bytes 737280 | tf_op jit(solution)/shard_map/all_gather | solution.py:83
  54.4 1.5 %copy.28 = bf16[128,2,1280]{2,1,0:T(2,128)(2,1)} copy(bf16[128,2,1280]{2,0,1:T(8,128)(2,1)S(1)} %all_gather.7) | data formatting | bytes 1310720 | tf_op jit(solution)/shard_map/all_gather | solution.py:83
  55.9 3.5 %all-to-all-start = ((bf16[128,2,1280]{2,1,0:T(2,128)(2,1)}), bf16[128,2,1280]{2,1,0:T(2,128)(2,1)S(1)}, u32[]{:S(2)}, u32[]{:S(2)}) async-start(bf16[128,2,1280]{2,1,0:T(2,128)(2,1)} %copy.28), calls=%async_computation | async-start | bytes 1310720 | tf_op jit(solution)/shard_map/all_to_all | solution.py:84
  59.4 10.2 %cosine_convert_fusion.1 = (bf16[640,801]{1,0:T(8,128)(2,1)S(1)}, bf16[640,801]{1,0:T(8,128)(2,1)S(1)}) fusion(s32[801]{0:T(1024)S(1)} %iota_add_fusion, s32[640]{0:T(1024)S(1)} %iota_add_fusion.1), kind=kLoop, calls=%fused_computation.41 | loop fusion | flops 6151680 | bytes 2056324 | tf_op jit(solution)/shard_map/convert
  69.6 6.8 %all_gather.6 = bf16[16,8,1280]{2,0,1:T(8,128)(2,1)S(1)} all-gather(bf16[16,2,1280]{2,0,1:T(8,128)(2,1)S(1)} %fusion.39), channel_id=1, replica_groups=mesh['row'=8,'col'=4] {'col'}, dimensions={1}, use_global_device_ids=true | all-gather | bytes 409600 | tf_op jit(solution)/shard_map/all_gather | solution.py:82
  76.4 1.6 %pad_maximum_fusion = bf16[1280,801]{1,0:T(8,128)(2,1)} fusion(bf16[640,801]{1,0:T(8,128)(2,1)S(1)} %get-tuple-element.59, bf16[640,801]{1,0:T(8,128)(2,1)S(1)} %get-tuple-element.58), kind=kLoop, calls=%fused_computation.39 | loop fusion | flops 4101120 | bytes 4101120 | tf_op jit(solution)/shard_map/concatenate | solution.py:26
  78.0 4.9 %copy.29 = bf16[32,4,2,1280]{0,2,1,3:T(2,128)(2,1)} copy(bf16[32,4,2,1280]{3,2,0,1:T(2,128)(2,1)S(1)} %bitcast.75) | data formatting | bytes 1310720 | tf_op jit(solution)/shard_map/all_to_all | solution.py:84
  82.9 46.5 %while.10 = (s32[]{:T(128)}, bf16[2,8,32,801]{3,2,1,0:T(8,128)(2,1)}, bf16[2,8,8,1280]{3,1,0,2:T(8,128)(2,1)S(1)}, bf16[32,8,1280]{0,1,2:T(8,128)(2,1)}, bf16[1280,801]{1,0:T(8,128)(2,1)}, /*index=5*/s32[]{:T(128)}) while((s32[]{:T(128)}, bf16[2,8,32,801]{3,2,1,0:T(8,128)(2,1)}, bf16[2,8,8,1280]{3,1,0,2:T(8,128)(2,1)S(1)}, ...), condition=%wide.region_2.3_spmd, body=%wide.region_1.2_spmd.sunk | while | flops 537149952 | bytes 34353424 | solution.py:92
  82.9 0.8 copy-done.3
  83.7 1.8 %copy.50 = bf16[1,8,8,1280]{2,1,3,0:T(8,128)(2,1)S(1)} copy(bf16[1,8,8,1280]{3,1,0,2:T(8,128)(2,1)S(1)} %constant_dynamic-slice_fusion.2) | data formatting | bytes 327680 | tf_op jit(solution)/shard_map/while/body/jit(dynamic_index_in_dim)/dynamic_slice | solution.py:92
  85.4 1.4 %fusion.98 = bf16[32,8,640]{0,1,2:T(8,128)(2,1)S(1)} fusion(bf16[32,8,1280]{0,1,2:T(8,128)(2,1)} %get-tuple-element.110), kind=kLoop, calls=%fused_computation.15.clone.1.clone.1 | loop fusion | bytes 655360 | tf_op jit(solution)/shard_map/while/body/eval_jaxpr/imf,jmf->ijf/dot_general | solution.py:55
  86.8 0.8 fusion.99
  87.7 0.9 copy-done
  88.6 0.1 fusion.100
  88.7 2.4 %add_bitcast_fusion.2 = f32[8,32,640]{1,0,2:T(8,128)} fusion(f32[640,8,32]{2,1,0:T(8,128)S(1)} %fusion.99, bf16[1,8,8,1280]{2,1,3,0:T(8,128)(2,1)S(1)} %copy.50, bf16[32,8,640]{0,1,2:T(8,128)(2,1)S(1)} %fusion.100), kind=kOutput, calls=%fused_computation.9.clone.2 | convolution fusion | flops 2785280 | bytes 1802240 | tf_op jit(solution)/shard_map/while/body/eval_jaxpr/imf,jmf->ijf/dot_general | solution.py:53
  91.0 3.0 %copy.52 = f32[8,32,640]{2,1,0:T(8,128)} copy(f32[8,32,640]{1,0,2:T(8,128)} %add_bitcast_fusion.2) | data formatting | bytes 1310720 | tf_op jit(solution)/shard_map/while/body/eval_jaxpr/add | solution.py:53
  94.1 1.4 %fusion.95 = bf16[32,8,640]{0,1,2:T(8,128)(2,1)S(1)} fusion(bf16[32,8,1280]{0,1,2:T(8,128)(2,1)} %get-tuple-element.110), kind=kLoop, calls=%fused_computation.16.clone.1.clone.1 | loop fusion | bytes 655360 | tf_op jit(solution)/shard_map/while/body/eval_jaxpr/imf,jmf->ijf/dot_general | solution.py:56
  95.5 0.8 fusion.96
  96.3 0.9 copy-done.1
  97.2 0.1 fusion.97
  97.3 2.4 %subtract_bitcast_fusion.2 = f32[8,32,640]{1,0,2:T(8,128)} fusion(f32[640,8,32]{2,1,0:T(8,128)S(1)} %fusion.96, bf16[1,8,8,1280]{2,1,3,0:T(8,128)(2,1)S(1)} %copy.50, bf16[32,8,640]{0,1,2:T(8,128)(2,1)S(1)} %fusion.97), kind=kOutput, calls=%fused_computation.8.clone.2 | convolution fusion | flops 2785280 | bytes 1802240 | tf_op jit(solution)/shard_map/while/body/eval_jaxpr/imf,jmf->ijf/dot_general | solution.py:58
  99.7 2.5 %copy.51 = f32[8,32,640]{2,1,0:T(8,128)S(1)} copy(f32[8,32,640]{1,0,2:T(8,128)} %subtract_bitcast_fusion.2) | data formatting | bytes 1310720 | tf_op jit(solution)/shard_map/while/body/eval_jaxpr/sub | solution.py:56
  102.2 2.7 %fusion.101 = bf16[256,801]{0,1:T(8,128)(2,1)S(1)} fusion(bf16[1280,801]{1,0:T(8,128)(2,1)} %get-tuple-element.111, f32[256,640]{1,0:T(8,128)S(1)} %bitcast.73, f32[256,640]{1,0:T(8,128)S(1)} %bitcast.72), kind=kOutput, calls=%fused_computation.13.clone.1 | convolution fusion | flops 526336512 | bytes 3771392 | tf_op jit(solution)/shard_map/while/body/eval_jaxpr/dot_general | solution.py:62
  104.9 0.2 copy.53
  105.2 0.9 copy-done.7
  106.2 0.8 copy-done.3
  106.9 1.8 %copy.50 = bf16[1,8,8,1280]{2,1,3,0:T(8,128)(2,1)S(1)} copy(bf16[1,8,8,1280]{3,1,0,2:T(8,128)(2,1)S(1)} %constant_dynamic-slice_fusion.2) | data formatting | bytes 327680 | tf_op jit(solution)/shard_map/while/body/jit(dynamic_index_in_dim)/dynamic_slice | solution.py:92
  108.7 1.4 %fusion.98 = bf16[32,8,640]{0,1,2:T(8,128)(2,1)S(1)} fusion(bf16[32,8,1280]{0,1,2:T(8,128)(2,1)} %get-tuple-element.110), kind=kLoop, calls=%fused_computation.15.clone.1.clone.1 | loop fusion | bytes 655360 | tf_op jit(solution)/shard_map/while/body/eval_jaxpr/imf,jmf->ijf/dot_general | solution.py:55
  110.1 0.8 fusion.99
  110.9 0.9 copy-done
  111.8 0.1 fusion.100
  111.9 2.4 %add_bitcast_fusion.2 = f32[8,32,640]{1,0,2:T(8,128)} fusion(f32[640,8,32]{2,1,0:T(8,128)S(1)} %fusion.99, bf16[1,8,8,1280]{2,1,3,0:T(8,128)(2,1)S(1)} %copy.50, bf16[32,8,640]{0,1,2:T(8,128)(2,1)S(1)} %fusion.100), kind=kOutput, calls=%fused_computation.9.clone.2 | convolution fusion | flops 2785280 | bytes 1802240 | tf_op jit(solution)/shard_map/while/body/eval_jaxpr/imf,jmf->ijf/dot_general | solution.py:53
  114.3 3.0 %copy.52 = f32[8,32,640]{2,1,0:T(8,128)} copy(f32[8,32,640]{1,0,2:T(8,128)} %add_bitcast_fusion.2) | data formatting | bytes 1310720 | tf_op jit(solution)/shard_map/while/body/eval_jaxpr/add | solution.py:53
  117.3 1.4 %fusion.95 = bf16[32,8,640]{0,1,2:T(8,128)(2,1)S(1)} fusion(bf16[32,8,1280]{0,1,2:T(8,128)(2,1)} %get-tuple-element.110), kind=kLoop, calls=%fused_computation.16.clone.1.clone.1 | loop fusion | bytes 655360 | tf_op jit(solution)/shard_map/while/body/eval_jaxpr/imf,jmf->ijf/dot_general | solution.py:56
  118.7 0.8 fusion.96
  119.6 0.9 copy-done.1
  120.6 2.4 %subtract_bitcast_fusion.2 = f32[8,32,640]{1,0,2:T(8,128)} fusion(f32[640,8,32]{2,1,0:T(8,128)S(1)} %fusion.96, bf16[1,8,8,1280]{2,1,3,0:T(8,128)(2,1)S(1)} %copy.50, bf16[32,8,640]{0,1,2:T(8,128)(2,1)S(1)} %fusion.97), kind=kOutput, calls=%fused_computation.8.clone.2 | convolution fusion | flops 2785280 | bytes 1802240 | tf_op jit(solution)/shard_map/while/body/eval_jaxpr/imf,jmf->ijf/dot_general | solution.py:58
  122.9 2.5 %copy.51 = f32[8,32,640]{2,1,0:T(8,128)S(1)} copy(f32[8,32,640]{1,0,2:T(8,128)} %subtract_bitcast_fusion.2) | data formatting | bytes 1310720 | tf_op jit(solution)/shard_map/while/body/eval_jaxpr/sub | solution.py:56
  125.5 2.7 %fusion.101 = bf16[256,801]{0,1:T(8,128)(2,1)S(1)} fusion(bf16[1280,801]{1,0:T(8,128)(2,1)} %get-tuple-element.111, f32[256,640]{1,0:T(8,128)S(1)} %bitcast.73, f32[256,640]{1,0:T(8,128)S(1)} %bitcast.72), kind=kOutput, calls=%fused_computation.13.clone.1 | convolution fusion | flops 526336512 | bytes 3771392 | tf_op jit(solution)/shard_map/while/body/eval_jaxpr/dot_general | solution.py:62
  128.2 0.2 copy.53
  128.5 0.9 copy-done.7
  (40 shorter events, 0.6 us)
Async XLA Ops:
  0.0 17.2 %copy-start.5 = (bf16[16,2,1500]{2,1,0:T(2,128)(2,1)S(1)}, bf16[16,2,1500]{2,1,0:T(2,128)(2,1)}, u32[]{:S(2)}) copy-start(bf16[16,2,1500]{2,1,0:T(2,128)(2,1)} %param.5) | copy-start | bytes 288004
  17.3 2.6 %copy-start.8 = (s32[128]{0:T(128)S(1)}, s32[128]{0:T(128)}, u32[]{:S(2)}) copy-start(s32[128]{0:T(128)} %param.6) | copy-start | bytes 1540
  17.3 2.7 %copy-start.9 = (s32[8]{0:T(128)S(1)}, s32[8]{0:T(128)}, u32[]{:S(2)}) copy-start(s32[8]{0:T(128)} %param.7) | copy-start | bytes 100
  55.9 22.1 %all-to-all-start = ((bf16[128,2,1280]{2,1,0:T(2,128)(2,1)}), bf16[128,2,1280]{2,1,0:T(2,128)(2,1)S(1)}, u32[]{:S(2)}, u32[]{:S(2)}) async-start(bf16[128,2,1280]{2,1,0:T(2,128)(2,1)} %copy.28), calls=%async_computation | async-start | bytes 1310720 | tf_op jit(solution)/shard_map/all_to_all | solution.py:84
  82.9 0.8 copy-start.3
  86.8 1.7 %copy-start = (bf16[32,8,1280]{0,1,2:T(8,128)(2,1)S(1)}, bf16[32,8,1280]{0,1,2:T(8,128)(2,1)}, u32[]{:S(2)}) copy-start(bf16[32,8,1280]{0,1,2:T(8,128)(2,1)} %get-tuple-element.110) | copy-start | bytes 1966084 | tf_op jit(solution)/shard_map/while
  95.5 1.7 %copy-start.1 = (bf16[32,8,1280]{0,1,2:T(8,128)(2,1)S(1)}, bf16[32,8,1280]{0,1,2:T(8,128)(2,1)}, u32[]{:S(2)}) copy-start(bf16[32,8,1280]{0,1,2:T(8,128)(2,1)} %get-tuple-element.110) | copy-start | bytes 1966084 | tf_op jit(solution)/shard_map/while
  99.7 2.5 %copy-start.2 = (f32[8,32,640]{2,1,0:T(8,128)S(1)}, f32[8,32,640]{2,1,0:T(8,128)}, u32[]{:S(2)}) copy-start(f32[8,32,640]{2,1,0:T(8,128)} %copy.52) | copy-start | bytes 1966084 | tf_op jit(solution)/shard_map/while
  102.2 3.0 %copy-start.6 = (bf16[2,8,32,801]{3,2,1,0:T(8,128)(2,1)S(1)}, bf16[2,8,32,801]{3,2,1,0:T(8,128)(2,1)}, u32[]{:S(2)}) copy-start(bf16[2,8,32,801]{3,2,1,0:T(8,128)(2,1)} %get-tuple-element.102) | copy-start | bytes 2460676 | tf_op jit(solution)/shard_map/while
  102.2 4.0 %copy-start.4 = (bf16[2,8,8,1280]{3,1,0,2:T(8,128)(2,1)S(1)}, bf16[2,8,8,1280]{3,1,0,2:T(8,128)(2,1)}, u32[]{:S(2)}) copy-start(bf16[2,8,8,1280]{3,1,0,2:T(8,128)(2,1)} %copy-done.3) | copy-start | bytes 983044 | tf_op jit(solution)/shard_map/while
  105.2 0.9 copy-start.7
  106.2 0.8 copy-start.3
  110.1 1.7 %copy-start = (bf16[32,8,1280]{0,1,2:T(8,128)(2,1)S(1)}, bf16[32,8,1280]{0,1,2:T(8,128)(2,1)}, u32[]{:S(2)}) copy-start(bf16[32,8,1280]{0,1,2:T(8,128)(2,1)} %get-tuple-element.110) | copy-start | bytes 1966084 | tf_op jit(solution)/shard_map/while
  118.7 1.7 %copy-start.1 = (bf16[32,8,1280]{0,1,2:T(8,128)(2,1)S(1)}, bf16[32,8,1280]{0,1,2:T(8,128)(2,1)}, u32[]{:S(2)}) copy-start(bf16[32,8,1280]{0,1,2:T(8,128)(2,1)} %get-tuple-element.110) | copy-start | bytes 1966084 | tf_op jit(solution)/shard_map/while
  122.9 2.5 %copy-start.2 = (f32[8,32,640]{2,1,0:T(8,128)S(1)}, f32[8,32,640]{2,1,0:T(8,128)}, u32[]{:S(2)}) copy-start(f32[8,32,640]{2,1,0:T(8,128)} %copy.52) | copy-start | bytes 1966084 | tf_op jit(solution)/shard_map/while
  125.4 3.0 %copy-start.6 = (bf16[2,8,32,801]{3,2,1,0:T(8,128)(2,1)S(1)}, bf16[2,8,32,801]{3,2,1,0:T(8,128)(2,1)}, u32[]{:S(2)}) copy-start(bf16[2,8,32,801]{3,2,1,0:T(8,128)(2,1)} %get-tuple-element.102) | copy-start | bytes 2460676 | tf_op jit(solution)/shard_map/while
  125.4 4.0 %copy-start.4 = (bf16[2,8,8,1280]{3,1,0,2:T(8,128)(2,1)S(1)}, bf16[2,8,8,1280]{3,1,0,2:T(8,128)(2,1)}, u32[]{:S(2)}) copy-start(bf16[2,8,8,1280]{3,1,0,2:T(8,128)(2,1)} %copy-done.3) | copy-start | bytes 983044 | tf_op jit(solution)/shard_map/while
  128.5 0.9 copy-start.7
where the time goes:
time: 130 us; the launch traced here: 129 us
  blocking collectives  40.2 us (31%)
  local copies, waits for them, and re-layouts  35.4 us (27%)
  other arithmetic  29.5 us (23%)
  matrix products  20.4 us (16%)
  starting transfers between devices  3.48 us (3%)
    all_gather x1, blocking collectives, body(): every_channel = lax.all_gather(local, 'row', axis=0, tiled=True)  33.5 us
    another operation x2, other arithmetic  27.4 us
    while x28, local copies, waits for them, and re-layouts  7.03 us
    all_gather x1, blocking collectives, body(): row_spectra = lax.all_gather(local, 'col', axis=1, tiled=True)  6.76 us
    add x2, local copies, waits for them, and re-layouts, correlate(): jnp.einsum('imf,jmf->ijf', row_real, col_real, preferred_element_type=jnp...  6.06 us
    dot_general x2, matrix products, correlate(): jnp.dot(stacked.reshape(-1, 2 * nfreq), itab, preferred_element_type=jnp....  5.41 us
    sub x2, local copies, waits for them, and re-layouts, correlate(): jnp.einsum('imf,jmf->ijf', row_imag, col_real, preferred_element_type=jnp...  4.94 us
    all_to_all x1, local copies, waits for them, and re-layouts, body(): lax.all_to_all(every_channel, 'col', split_axis=0, concat_axis=1, tiled=T...  4.91 us
  transfers between devices with their start and end apart: 1, of which 0 were waited for; matrix products, arithmetic and copies ran while one was open for 9% of the time, Pallas kernels for 0%

commit v1 on v0

v1 whole, which is shorter than its diff:
```python
import functools
import math

import jax
import jax.numpy as jnp
import numpy as np
from jax import lax
from jax.experimental import pallas as pl
from jax.experimental.pallas import tpu as pltpu
from jax.sharding import PartitionSpec as P

F = 640
BAND = 32
MAXLAG = 400
LANES = 128
MESH = pl.DeviceIdType.MESH


def forward_table(length, nfreq, padded):
    times = np.arange(length, dtype=np.int64)[:, None]
    freqs = np.arange(1, nfreq + 1, dtype=np.int64)[None, :]
    phase = (times * freqs % length).astype(np.float32) * np.float32(2.0 * math.pi / length)
    table = np.concatenate([np.cos(phase), -np.sin(phase)], axis=1)
    return np.pad(table, ((0, padded - length), (0, 0))).astype(jnp.bfloat16)


def inverse_table(length, nfreq, maxlag, padded):
    freqs = np.arange(1, nfreq + 1, dtype=np.int64)[:, None]
    shifts = np.arange(-maxlag, maxlag + 1, dtype=np.int64)[None, :]
    phase = np.mod(freqs * shifts, length).astype(np.float32) * np.float32(2.0 * math.pi / length)
    table = np.concatenate([np.cos(phase), -np.sin(phase)], axis=0)
    return np.pad(table, ((0, 0), (0, padded - table.shape[1]))).astype(jnp.bfloat16)


def kernel(
    rows_n, cols_n, rc, pm,
    rec_ref, ftab_hbm, itab_hbm, out_ref,
    ftab, itab, spec, rowb, colb, rowf, colf, stacked,
    tab_sem, z_send, z_recv, r_send, r_recv, c_send, c_recv,
):
    k = rows_n // cols_n
    me_r = lax.axis_index("row")
    me_c = lax.axis_index("col")
    me_q = me_r // k
    me_s = lax.rem(me_r, k)
    minutes = pm * cols_n
    jc = k * rc

    f_copy = pltpu.make_async_copy(ftab_hbm, ftab, tab_sem.at[0])
    i_copy = pltpu.make_async_copy(itab_hbm, itab, tab_sem.at[1])
    f_copy.start()
    i_copy.start()

    barrier = pltpu.get_barrier_semaphore()
    peers = []
    for d in range(1, cols_n):
        peers.append((lax.rem(me_q + d, cols_n) * k + me_s, me_c))
    for e in range(k):
        for d in range(cols_n):
            if e or d:
                peers.append((me_q * k + lax.rem(me_s + e, k), lax.rem(me_c + d, cols_n)))
    for peer in peers:
        pl.semaphore_signal(barrier, inc=1, device_id=peer, device_id_type=MESH)

    f_copy.wait()
    raw = jnp.dot(rec_ref[...], ftab[...], preferred_element_type=jnp.float32)
    re = raw[:, :F]
    im = raw[:, F:]
    sq = re * re + im * im
    nv = F // LANES
    n = pm * rc
    sq = jnp.concatenate([sq[:, v * LANES:(v + 1) * LANES] for v in range(nv)], axis=0)
    shift = int(math.log2(BAND))
    same = (lax.broadcasted_iota(jnp.int32, (LANES, LANES), 0) >> shift) == (
        lax.broadcasted_iota(jnp.int32, (LANES, LANES), 1) >> shift
    )
    ones = jnp.where(same, 1.0, 0.0).astype(jnp.bfloat16)
    hi = sq.astype(jnp.bfloat16)
    rest = sq - hi.astype(jnp.float32)
    mid = rest.astype(jnp.bfloat16)
    low = (rest - mid.astype(jnp.float32)).astype(jnp.bfloat16)
    power = (
        jnp.dot(hi, ones, preferred_element_type=jnp.float32)
        + jnp.dot(mid, ones, preferred_element_type=jnp.float32)
        + jnp.dot(low, ones, preferred_element_type=jnp.float32)
    ) * jnp.float32(1.0 / (2 * BAND))
    weight = lax.rsqrt(power + 1e-06)
    weight = jnp.concatenate([weight[v * n:(v + 1) * n] for v in range(nv)], axis=1)
    white_re = (re * weight).astype(jnp.bfloat16)
    white_im = (im * weight).astype(jnp.bfloat16)
    for m in range(pm):
        spec[me_q, m, :, :F] = white_re[m * rc:(m + 1) * rc]
        spec[me_q, m, :, F:] = white_im[m * rc:(m + 1) * rc]

    pl.semaphore_wait(barrier, len(peers))

    sends = []
    for d in range(1, cols_n):
        to_q = lax.rem(me_q + d, cols_n)
        copy = pltpu.make_async_remote_copy(
            spec.at[me_q], spec.at[me_q], z_send.at[d], z_recv.at[me_q],
            device_id=(to_q * k + me_s, me_c), device_id_type=MESH,
        )
        copy.start()
        sends.append(copy)
    for d in range(1, cols_n):
        to_c = lax.rem(me_c + d, cols_n)
        copy = pltpu.make_async_remote_copy(
            spec.at[me_q], rowb.at[me_c], r_send.at[d], r_recv.at[me_c],
            device_id=(me_r, to_c), device_id_type=MESH,
        )
        copy.start()
        sends.append(copy)
    rowb[me_c] = spec[me_q]
    guarded = []
    for d in range(cols_n):
        q = lax.rem(me_q + d, cols_n)
        if d:
            pltpu.make_async_remote_copy(
                spec.at[q], spec.at[q], z_send.at[d], z_recv.at[q],
                device_id=(q * k + me_s, me_c), device_id_type=MESH,
            ).wait_recv()
        for e in range(k):
            copy = pltpu.make_async_remote_copy(
                spec.at[q], colb.at[me_s, me_c], c_send.at[d, e], c_recv.at[me_s, me_c],
                device_id=(me_q * k + lax.rem(me_s + e, k), q), device_id_type=MESH,
            )
            if e:
                copy.start()
                sends.append(copy)
            else:
                @pl.when(q != me_c)
                def _():
                    copy.start()

                @pl.when(q == me_c)
                def _():
                    colb[me_s, me_c] = spec[q]
                guarded.append((q, copy))

    for d in range(cols_n):
        c = lax.rem(me_c + d, cols_n)
        if d:
            pltpu.make_async_remote_copy(
                spec.at[me_q], rowb.at[c], r_send.at[d], r_recv.at[c],
                device_id=(me_r, c), device_id_type=MESH,
            ).wait_recv()
        for m in range(pm):
            rowf[:, d * pm + m, :] = rowb[c, m].astype(jnp.float32)
    for e in range(k):
        s = lax.rem(me_s + e, k)
        for d in range(cols_n):
            c = lax.rem(me_c + d, cols_n)
            if e or d:
                pltpu.make_async_remote_copy(
                    spec.at[me_q], colb.at[s, c], c_send.at[d, e], c_recv.at[s, c],
                    device_id=(me_q * k + s, c), device_id_type=MESH,
                ).wait_recv()
            for m in range(pm):
                colf[d * pm + m, pl.ds(pl.multiple_of(s * rc, rc), rc), :] = (
                    colb[s, c, m].astype(jnp.float32)
                )

    i_copy.wait()
    scale = jnp.float32(1.0 / minutes)
    step = 2

    def pair(p, carry):
        for v in range(nv):
            lo = v * LANES
            hi_ = F + v * LANES
            acc = [[None, None] for _ in range(step)]
            for m in range(minutes):
                cr = colf[m, :, lo:lo + LANES]
                ci = colf[m, :, hi_:hi_ + LANES]
                for u in range(step):
                    rr = rowf[p * step + u, m:m + 1, lo:lo + LANES]
                    ri = rowf[p * step + u, m:m + 1, hi_:hi_ + LANES]
                    real = rr * cr + ri * ci
                    imag = ri * cr - rr * ci
                    acc[u][0] = real if m == 0 else acc[u][0] + real
                    acc[u][1] = imag if m == 0 else acc[u][1] + imag
            for u in range(step):
                stacked[p * step + u, :, lo:lo + LANES] = (acc[u][0] * scale).astype(jnp.bfloat16)
                stacked[p * step + u, :, hi_:hi_ + LANES] = (acc[u][1] * scale).astype(jnp.bfloat16)
        return carry

    lax.fori_loop(0, rc // step, pair, 0)

    group = 256 // jc
    lags = out_ref.shape[2]

    def lagged(b, carry):
        left = stacked[pl.ds(b * group, group)].reshape(group * jc, 2 * F)
        result = jnp.dot(left, itab[...], preferred_element_type=jnp.float32)
        result = (result * jnp.float32(1.0 / math.sqrt(F))).astype(jnp.bfloat16)
        out_ref[pl.ds(b * group, group)] = result[:, :lags].reshape(group, jc, lags)
        return carry

    lax.fori_loop(0, rc // group, lagged, 0)

    for copy in sends:
        copy.wait_send()
    for q, copy in guarded:
        @pl.when(q != me_c)
        def _():
            copy.wait_send()


def body(rows_n, cols_n, records, channel_live, minute_valid):
    rc, pm, length = records.shape
    padded = -(-length // 256) * 256
    lags = 2 * MAXLAG + 1
    lag_pad = -(-lags // LANES) * LANES
    k = rows_n // cols_n
    minutes = pm * cols_n
    live = lax.dynamic_slice_in_dim(channel_live, lax.axis_index("row") * rc, rc)
    valid = lax.dynamic_slice_in_dim(minute_valid, lax.axis_index("col") * pm, pm)
    keep = (live[:, None] * valid[None, :]).astype(jnp.bfloat16)
    rec = (records * keep[:, :, None]).transpose(1, 0, 2)
    rec = jnp.pad(rec, ((0, 0), (0, 0), (0, padded - length))).reshape(pm * rc, padded)
    ftab = jnp.asarray(forward_table(length, F, padded))
    itab = jnp.asarray(inverse_table(length, F, MAXLAG, lag_pad))
    jc = k * rc
    return pl.pallas_call(
        functools.partial(kernel, rows_n, cols_n, rc, pm),
        out_shape=jax.ShapeDtypeStruct((rc, jc, lags), jnp.bfloat16),
        in_specs=[
            pl.BlockSpec(memory_space=pltpu.VMEM),
            pl.BlockSpec(memory_space=pl.ANY),
            pl.BlockSpec(memory_space=pl.ANY),
        ],
        out_specs=pl.BlockSpec(memory_space=pltpu.VMEM),
        scratch_shapes=[
            pltpu.VMEM((padded, 2 * F), jnp.bfloat16),
            pltpu.VMEM((2 * F, lag_pad), jnp.bfloat16),
            pltpu.VMEM((cols_n, pm, rc, 2 * F), jnp.bfloat16),
            pltpu.VMEM((cols_n, pm, rc, 2 * F), jnp.bfloat16),
            pltpu.VMEM((k, cols_n, pm, rc, 2 * F), jnp.bfloat16),
            pltpu.VMEM((rc, minutes, 2 * F), jnp.float32),
            pltpu.VMEM((minutes, jc, 2 * F), jnp.float32),
            pltpu.VMEM((rc, jc, 2 * F), jnp.bfloat16),
            pltpu.SemaphoreType.DMA((2,)),
            pltpu.SemaphoreType.DMA((cols_n,)),
            pltpu.SemaphoreType.DMA((cols_n,)),
            pltpu.SemaphoreType.DMA((cols_n,)),
            pltpu.SemaphoreType.DMA((cols_n,)),
            pltpu.SemaphoreType.DMA((cols_n, k)),
            pltpu.SemaphoreType.DMA((k, cols_n)),
        ],
        compiler_params=pltpu.CompilerParams(
            collective_id=0, has_side_effects=True, vmem_limit_bytes=56 * 1024 * 1024
        ),
    )(rec, ftab, itab)


def solution(mesh):
    in_specs = (P("row", "col", None), P(), P())
    out_specs = P("row", "col", None)
    run = functools.partial(body, mesh.shape["row"], mesh.shape["col"])
    return jax.shard_map(run, mesh=mesh, in_specs=in_specs, out_specs=out_specs, check_vma=False)
```

time: 130 us -> 32.7 us (0.25)
  the two profiles are of different devices: /device:TPU:0 before, /device:TPU:8 now
where the time goes in v1:
time: 32.7 us; the launch traced here: 32.5 us
  Pallas kernels  27 us (83%)
  local copies, waits for them, and re-layouts  4.39 us (13%)
  other arithmetic  1.12 us (3%)
    pallas_call x1, Pallas kernels, body(): pl.pallas_call(functools.partial(kernel, rows_n, cols_n, rc, pm), out_sha...  27 us
    unnamed x2, local copies, waits for them, and re-layouts  2.19 us
    transpose x1, other arithmetic, body(): rec = (records * keep[:, :, None]).transpose(1, 0, 2)  1.05 us
    dynamic_slice x1, local copies, waits for them, and re-layouts, body(): lax.dynamic_slice_in_dim(minute_valid, lax.axis_index('col') * pm, pm)  0.73 us
    dynamic_slice x1, local copies, waits for them, and re-layouts, body(): lax.dynamic_slice_in_dim(channel_live, lax.axis_index('row') * rc, rc)  0.73 us

profile of v1, /device:TPU:8, one launch (start us, length us, event | category | flops | bytes accessed | tf_op | source)
XLA Modules:
  0.0 32.5 jit_solution(9371428721621016150)
XLA Ops:
  0.0 0.7 %dynamic_slice.7 = s32[2]{0:T(128)S(1)} dynamic-slice(s32[8]{0:T(128)} %param.7, s32[]{:T(128)S(6)} %select_n.7), dynamic_slice_sizes={2} | dynamic-slice | bytes 20 | tf_op jit(solution)/shard_map/dynamic_slice | solution.py:218
  0.7 0.7 %dynamic_slice.6 = s32[16]{0:T(128)S(1)} dynamic-slice(s32[128]{0:T(128)} %param.6, s32[]{:T(128)S(6)} %select_n.6), dynamic_slice_sizes={16} | dynamic-slice | bytes 132 | tf_op jit(solution)/shard_map/dynamic_slice | solution.py:217
  1.5 0.1 multiply_convert_fusion
  1.5 0.1 copy.7
  1.6 1.0 %multiply_bitcast_fusion = bf16[2,16,1500]{2,0,1:T(2,128)(2,1)S(1)} fusion(bf16[16,2,1500]{2,1,0:T(2,128)(2,1)} %param.5, bf16[16,2]{1,0:T(8,128)(2,1)S(1)} %copy.7), kind=kLoop, calls=%fused_computation | loop fusion | flops 48000 | bytes 192064 | tf_op jit(solution)/shard_map/transpose | solution.py:220
  2.7 0.7 %pad.4.clone = bf16[2,16,1536]{2,1,0:T(8,128)(2,1)} pad(bf16[2,16,1500]{2,1,0:T(8,128)(2,1)S(1)} %copy.9, bf16[]{:T(256)} %constant.24.clone.1), padding=0_0x0_0x0_36 | pad | bytes 194306 | tf_op jit(solution)/shard_map/jit(_pad)/pad | solution.py:221
  3.4 27.0 %shard_map.55 = bf16[16,32,801]{2,1,0:T(8,128)(2,1)} custom-call(bf16[32,1536]{1,0:T(8,128)(2,1)} %bitcast.3, bf16[1536,1280]{1,0:T(8,128)(2,1)} %constant.25.clone.ftab_hbm, bf16[1280,896]{1,0:T(8,128)(2,1)} %constant.26.clone.itab_hbm), custom_call_target="tpu_custom_call" | custom-call | tf_op jit(solution)/shard_map/pallas_call | solution.py:225
  30.3 2.2 %copy.11 = bf16[16,32,801]{2,1,0:T(8,128)(2,1)} copy(bf16[16,32,801]{2,1,0:T(8,128)(2,1)} %shard_map.55) | data formatting | bytes 1640448
  (1 shorter events, 0.0 us)

commit v2 on v1

--- a/solution.py
+++ b/solution.py
@@ -34,8 +34,8 @@
 
 def kernel(
     rows_n, cols_n, rc, pm,
-    rec_ref, ftab_hbm, itab_hbm, out_ref,
-    ftab, itab, spec, rowb, colb, rowf, colf, stacked,
+    live_ref, valid_ref, rec_ref, ftab_hbm, itab_hbm, out_ref,
+    ftab, itab, spec, rowb, colb, rowf, colf, stacked, white,
     tab_sem, z_send, z_recv, r_send, r_recv, c_send, c_recv,
 ):
     k = rows_n // cols_n
@@ -63,7 +63,7 @@
         pl.semaphore_signal(barrier, inc=1, device_id=peer, device_id_type=MESH)
 
     f_copy.wait()
-    raw = jnp.dot(rec_ref[...], ftab[...], preferred_element_type=jnp.float32)
+    raw = jnp.dot(rec_ref[...].reshape(pm * rc, rec_ref.shape[2]), ftab[...], preferred_element_type=jnp.float32)
     re = raw[:, :F]
     im = raw[:, F:]
     sq = re * re + im * im
@@ -86,11 +86,21 @@
     ) * jnp.float32(1.0 / (2 * BAND))
     weight = lax.rsqrt(power + 1e-06)
     weight = jnp.concatenate([weight[v * n:(v + 1) * n] for v in range(nv)], axis=1)
-    white_re = (re * weight).astype(jnp.bfloat16)
-    white_im = (im * weight).astype(jnp.bfloat16)
+    row_at = lax.broadcasted_iota(jnp.int32, (rc, 1), 0)
+    live = jnp.zeros((rc, 1), jnp.int32)
+    for i in range(rc):
+        live = jnp.where(row_at == i, live_ref[me_r * rc + i], live)
+    live = live.astype(jnp.float32)
+    for v in range(nv):
+        at = slice(v * LANES, (v + 1) * LANES)
+        white[v] = re[:, at] * weight[:, at]
+        white[nv + v] = im[:, at] * weight[:, at]
     for m in range(pm):
-        spec[me_q, m, :, :F] = white_re[m * rc:(m + 1) * rc]
-        spec[me_q, m, :, F:] = white_im[m * rc:(m + 1) * rc]
+        keep = live * valid_ref[me_c * pm + m].astype(jnp.float32)
+        for v in range(2 * nv):
+            spec[me_q, m, :, v * LANES:(v + 1) * LANES] = (
+                white[v, pl.ds(m, rc, stride=pm), :] * keep
+            ).astype(jnp.bfloat16)
 
     pl.semaphore_wait(barrier, len(peers))
 
@@ -209,30 +219,26 @@
 
 def body(rows_n, cols_n, records, channel_live, minute_valid):
     rc, pm, length = records.shape
-    padded = -(-length // 256) * 256
     lags = 2 * MAXLAG + 1
     lag_pad = -(-lags // LANES) * LANES
     k = rows_n // cols_n
     minutes = pm * cols_n
-    live = lax.dynamic_slice_in_dim(channel_live, lax.axis_index("row") * rc, rc)
-    valid = lax.dynamic_slice_in_dim(minute_valid, lax.axis_index("col") * pm, pm)
-    keep = (live[:, None] * valid[None, :]).astype(jnp.bfloat16)
-    rec = (records * keep[:, :, None]).transpose(1, 0, 2)
-    rec = jnp.pad(rec, ((0, 0), (0, 0), (0, padded - length))).reshape(pm * rc, padded)
-    ftab = jnp.asarray(forward_table(length, F, padded))
+    ftab = jnp.asarray(forward_table(length, F, length))
     itab = jnp.asarray(inverse_table(length, F, MAXLAG, lag_pad))
     jc = k * rc
     return pl.pallas_call(
         functools.partial(kernel, rows_n, cols_n, rc, pm),
         out_shape=jax.ShapeDtypeStruct((rc, jc, lags), jnp.bfloat16),
         in_specs=[
+            pl.BlockSpec(memory_space=pltpu.SMEM),
+            pl.BlockSpec(memory_space=pltpu.SMEM),
             pl.BlockSpec(memory_space=pltpu.VMEM),
             pl.BlockSpec(memory_space=pl.ANY),
             pl.BlockSpec(memory_space=pl.ANY),
         ],
         out_specs=pl.BlockSpec(memory_space=pltpu.VMEM),
         scratch_shapes=[
-            pltpu.VMEM((padded, 2 * F), jnp.bfloat16),
+            pltpu.VMEM((length, 2 * F), jnp.bfloat16),
             pltpu.VMEM((2 * F, lag_pad), jnp.bfloat16),
             pltpu.VMEM((cols_n, pm, rc, 2 * F), jnp.bfloat16),
             pltpu.VMEM((cols_n, pm, rc, 2 * F), jnp.bfloat16),
@@ -240,6 +246,7 @@
             pltpu.VMEM((rc, minutes, 2 * F), jnp.float32),
             pltpu.VMEM((minutes, jc, 2 * F), jnp.float32),
             pltpu.VMEM((rc, jc, 2 * F), jnp.bfloat16),
+            pltpu.VMEM((2 * F // LANES, pm * rc, LANES), jnp.float32),
             pltpu.SemaphoreType.DMA((2,)),
             pltpu.SemaphoreType.DMA((cols_n,)),
             pltpu.SemaphoreType.DMA((cols_n,)),
@@ -251,7 +258,7 @@
         compiler_params=pltpu.CompilerParams(
             collective_id=0, has_side_effects=True, vmem_limit_bytes=56 * 1024 * 1024
         ),
-    )(rec, ftab, itab)
+    )(channel_live, minute_valid, records, ftab, itab)
 
 
 def solution(mesh):

time: 32.7 us -> 29.3 us (0.90)
  local copies, waits for them, and re-layouts: 4.39 us -> 2.18 us
  other arithmetic: 1.12 us -> 0 us
    dynamic_slice x2 -> x0, local copies, waits for them, and re-layouts: 1.45 us -> none  [the longest x1 0.73 us: body(): lax.dynamic_slice_in_dim(minute_valid, lax.axis_index('col') * pm, pm)]
    transpose x1 -> x0, other arithmetic: 1.05 us -> none  [body(): rec = (records * keep[:, :, None]).transpose(1, 0, 2)]
    pad x1 -> x0, local copies, waits for them, and re-layouts: 0.65 us -> none  [body(): jnp.pad(rec, ((0, 0), (0, 0), (0, padded - length)))]
    unnamed x2 -> x1, local copies, waits for them, and re-layouts: 2.19 us -> 2.18 us
where the time goes in v2:
time: 29.3 us; the launch traced here: 29.1 us
  Pallas kernels  26.9 us (92%)
  local copies, waits for them, and re-layouts  2.18 us (7%)
    pallas_call x1, Pallas kernels, body(): pl.pallas_call(functools.partial(kernel, rows_n, cols_n, rc, pm), out_sha...  26.9 us
    unnamed x1, local copies, waits for them, and re-layouts  2.18 us

profile of v2, /device:TPU:8, one launch (start us, length us, event | category | flops | bytes accessed | tf_op | source)
XLA Modules:
  0.0 29.1 jit_solution(2942347201600730125)
XLA Ops:
  0.0 26.9 %shard_map.55 = bf16[16,32,801]{2,1,0:T(8,128)(2,1)} custom-call(s32[128]{0:T(128)} %live_ref.1, s32[8]{0:T(128)} %valid_ref.1, bf16[16,2,1500]{2,1,0:T(2,128)(2,1)} %rec_ref.1, bf16[1500,1280]{1,0:T(8,128)(2,1)} %constant.4.clone.ftab_hbm, bf16[1280,896]{1,0:T(8,128)(2,1)} %constant.5.clone.itab_hbm), custom_call_target="tpu_custom_call" | custom-call | tf_op jit(solution)/shard_map/pallas_call | solution.py:229
  26.9 2.2 %copy.7 = bf16[16,32,801]{2,1,0:T(8,128)(2,1)} copy(bf16[16,32,801]{2,1,0:T(8,128)(2,1)} %shard_map.55) | data formatting | bytes 1640448

commit v3 on v2

--- a/solution.py
+++ b/solution.py
@@ -36,7 +36,7 @@
     rows_n, cols_n, rc, pm,
     live_ref, valid_ref, rec_ref, ftab_hbm, itab_hbm, out_ref,
     ftab, itab, spec, rowb, colb, rowf, colf, stacked, white,
-    tab_sem, z_send, z_recv, r_send, r_recv, c_send, c_recv,
+    tab_sem, z_send, z_recv, r_send, r_recv, b_send, c_recv,
 ):
     k = rows_n // cols_n
     me_r = lax.axis_index("row")
@@ -51,16 +51,33 @@
     f_copy.start()
     i_copy.start()
 
+    def start_if(cond, copy, waits):
+        if cond is None:
+            copy.start()
+        else:
+            pl.when(cond)(copy.start)
+        waits.append((cond, copy))
+
+    above = me_q + 1 < cols_n
+    below = me_q > 0
+    up = jnp.minimum(me_q + 1, cols_n - 1) * k + me_s
+    down = jnp.maximum(me_q - 1, 0) * k + me_s
     barrier = pltpu.get_barrier_semaphore()
     peers = []
-    for d in range(1, cols_n):
-        peers.append((lax.rem(me_q + d, cols_n) * k + me_s, me_c))
     for e in range(k):
         for d in range(cols_n):
             if e or d:
                 peers.append((me_q * k + lax.rem(me_s + e, k), lax.rem(me_c + d, cols_n)))
     for peer in peers:
         pl.semaphore_signal(barrier, inc=1, device_id=peer, device_id_type=MESH)
+
+    @pl.when(above)
+    def _():
+        pl.semaphore_signal(barrier, inc=1, device_id=(up, me_c), device_id_type=MESH)
+
+    @pl.when(below)
+    def _():
+        pl.semaphore_signal(barrier, inc=1, device_id=(down, me_c), device_id_type=MESH)
 
     f_copy.wait()
     raw = jnp.dot(rec_ref[...].reshape(pm * rc, rec_ref.shape[2]), ftab[...], preferred_element_type=jnp.float32)
@@ -102,58 +119,76 @@
                 white[v, pl.ds(m, rc, stride=pm), :] * keep
             ).astype(jnp.bfloat16)
 
-    pl.semaphore_wait(barrier, len(peers))
-
-    sends = []
+    pl.semaphore_wait(
+        barrier, len(peers) + above.astype(jnp.int32) + below.astype(jnp.int32)
+    )
+
+    def remote(src, dst, send, recv, device):
+        return pltpu.make_async_remote_copy(
+            src, dst, send, recv, device_id=device, device_id_type=MESH
+        )
+
+    waits = []
+    parts = 2
+    size = pm // parts
+
+    def cut(part):
+        return pl.ds(part * size, size)
+
+    def hop(q, way, part):
+        return remote(
+            spec.at[q, cut(part)], spec.at[q, cut(part)], z_send.at[q, way, part], z_recv.at[q, part],
+            (down if way else up, me_c),
+        )
+
+    def to_block(q, cond, part):
+        other = q != me_c
+        if cond is not None:
+            other = jnp.logical_and(cond, other)
+        for e in range(k):
+            start_if(
+                cond if e else other,
+                remote(
+                    spec.at[q, cut(part)], colb.at[me_s, me_c, cut(part)],
+                    b_send.at[q, e, part], c_recv.at[me_s, me_c, part],
+                    (me_q * k + lax.rem(me_s + e, k), q),
+                ),
+                waits,
+            )
+
+    for part in range(parts):
+        start_if(above, hop(me_q, 0, part), waits)
+        start_if(below, hop(me_q, 1, part), waits)
+        to_block(me_q, None, part)
     for d in range(1, cols_n):
-        to_q = lax.rem(me_q + d, cols_n)
-        copy = pltpu.make_async_remote_copy(
-            spec.at[me_q], spec.at[me_q], z_send.at[d], z_recv.at[me_q],
-            device_id=(to_q * k + me_s, me_c), device_id_type=MESH,
+        start_if(
+            None,
+            remote(
+                spec.at[me_q], rowb.at[me_c], r_send.at[d], r_recv.at[me_c],
+                (me_r, lax.rem(me_c + d, cols_n)),
+            ),
+            waits,
         )
-        copy.start()
-        sends.append(copy)
+    rowb[me_c] = spec[me_q]
     for d in range(1, cols_n):
-        to_c = lax.rem(me_c + d, cols_n)
-        copy = pltpu.make_async_remote_copy(
-            spec.at[me_q], rowb.at[me_c], r_send.at[d], r_recv.at[me_c],
-            device_id=(me_r, to_c), device_id_type=MESH,
-        )
-        copy.start()
-        sends.append(copy)
-    rowb[me_c] = spec[me_q]
-    guarded = []
-    for d in range(cols_n):
-        q = lax.rem(me_q + d, cols_n)
-        if d:
-            pltpu.make_async_remote_copy(
-                spec.at[q], spec.at[q], z_send.at[d], z_recv.at[q],
-                device_id=(q * k + me_s, me_c), device_id_type=MESH,
-            ).wait_recv()
-        for e in range(k):
-            copy = pltpu.make_async_remote_copy(
-                spec.at[q], colb.at[me_s, me_c], c_send.at[d, e], c_recv.at[me_s, me_c],
-                device_id=(me_q * k + lax.rem(me_s + e, k), q), device_id_type=MESH,
-            )
-            if e:
-                copy.start()
-                sends.append(copy)
-            else:
-                @pl.when(q != me_c)
-                def _():
-                    copy.start()
-
-                @pl.when(q == me_c)
-                def _():
-                    colb[me_s, me_c] = spec[q]
-                guarded.append((q, copy))
+        low_ok = me_q >= d
+        low_q = jnp.maximum(me_q - d, 0)
+        high_ok = me_q + d < cols_n
+        high_q = jnp.minimum(me_q + d, cols_n - 1)
+        for part in range(parts):
+            pl.when(low_ok)(hop(low_q, 0, part).wait_recv)
+            start_if(jnp.logical_and(low_ok, above), hop(low_q, 0, part), waits)
+            to_block(low_q, low_ok, part)
+            pl.when(high_ok)(hop(high_q, 1, part).wait_recv)
+            start_if(jnp.logical_and(high_ok, below), hop(high_q, 1, part), waits)
+            to_block(high_q, high_ok, part)
+    colb[me_s, me_c] = spec[me_c]
 
     for d in range(cols_n):
         c = lax.rem(me_c + d, cols_n)
         if d:
-            pltpu.make_async_remote_copy(
-                spec.at[me_q], rowb.at[c], r_send.at[d], r_recv.at[c],
-                device_id=(me_r, c), device_id_type=MESH,
+            remote(
+                spec.at[me_q], rowb.at[c], r_send.at[d], r_recv.at[c], (me_r, c)
             ).wait_recv()
         for m in range(pm):
             rowf[:, d * pm + m, :] = rowb[c, m].astype(jnp.float32)
@@ -162,10 +197,11 @@
         for d in range(cols_n):
             c = lax.rem(me_c + d, cols_n)
             if e or d:
-                pltpu.make_async_remote_copy(
-                    spec.at[me_q], colb.at[s, c], c_send.at[d, e], c_recv.at[s, c],
-                    device_id=(me_q * k + s, c), device_id_type=MESH,
-                ).wait_recv()
+                for part in range(parts):
+                    remote(
+                        spec.at[me_q, cut(part)], colb.at[s, c, cut(part)],
+                        b_send.at[me_q, e, part], c_recv.at[s, c, part], (me_q * k + s, c),
+                    ).wait_recv()
             for m in range(pm):
                 colf[d * pm + m, pl.ds(pl.multiple_of(s * rc, rc), rc), :] = (
                     colb[s, c, m].astype(jnp.float32)
@@ -209,12 +245,11 @@
 
     lax.fori_loop(0, rc // group, lagged, 0)
 
-    for copy in sends:
-        copy.wait_send()
-    for q, copy in guarded:
-        @pl.when(q != me_c)
-        def _():
+    for cond, copy in waits:
+        if cond is None:
             copy.wait_send()
+        else:
+            pl.when(cond)(copy.wait_send)
 
 
 def body(rows_n, cols_n, records, channel_live, minute_valid):
@@ -248,12 +283,12 @@
             pltpu.VMEM((rc, jc, 2 * F), jnp.bfloat16),
             pltpu.VMEM((2 * F // LANES, pm * rc, LANES), jnp.float32),
             pltpu.SemaphoreType.DMA((2,)),
+            pltpu.SemaphoreType.DMA((cols_n, 2, 2)),
+            pltpu.SemaphoreType.DMA((cols_n, 2)),
             pltpu.SemaphoreType.DMA((cols_n,)),
             pltpu.SemaphoreType.DMA((cols_n,)),
-            pltpu.SemaphoreType.DMA((cols_n,)),
-            pltpu.SemaphoreType.DMA((cols_n,)),
-            pltpu.SemaphoreType.DMA((cols_n, k)),
-            pltpu.SemaphoreType.DMA((k, cols_n)),
+            pltpu.SemaphoreType.DMA((cols_n, k, 2)),
+            pltpu.SemaphoreType.DMA((k, cols_n, 2)),
         ],
         compiler_params=pltpu.CompilerParams(
             collective_id=0, has_side_effects=True, vmem_limit_bytes=56 * 1024 * 1024

time: 29.3 us -> 27 us (0.922)
  the two profiles are of different devices: /device:TPU:8 before, /device:TPU:5 now
where the time goes in v3:
time: 27 us; the launch traced here: 26.9 us
  Pallas kernels  24.7 us (91%)
  local copies, waits for them, and re-layouts  2.18 us (8%)
    pallas_call x1, Pallas kernels, body(): pl.pallas_call(functools.partial(kernel, rows_n, cols_n, rc, pm), out_sha...  24.7 us
    unnamed x1, local copies, waits for them, and re-layouts  2.18 us

profile of v3, /device:TPU:5, one launch (start us, length us, event | category | flops | bytes accessed | tf_op | source)
XLA Modules:
  0.0 26.9 jit_solution(13166948946851495914)
XLA Ops:
  0.0 24.7 %shard_map.55 = bf16[16,32,801]{2,1,0:T(8,128)(2,1)} custom-call(s32[128]{0:T(128)} %live_ref.1, s32[8]{0:T(128)} %valid_ref.1, bf16[16,2,1500]{2,1,0:T(2,128)(2,1)} %rec_ref.1, bf16[1500,1280]{1,0:T(8,128)(2,1)} %constant.4.clone.ftab_hbm, bf16[1280,896]{1,0:T(8,128)(2,1)} %constant.5.clone.itab_hbm), custom_call_target="tpu_custom_call" | custom-call | tf_op jit(solution)/shard_map/pallas_call | solution.py:264
  24.7 2.2 %copy.7 = bf16[16,32,801]{2,1,0:T(8,128)(2,1)} copy(bf16[16,32,801]{2,1,0:T(8,128)(2,1)} %shard_map.55) | data formatting | bytes 1640448
